TPU v7x, 256 devices: a whole 4x4x8 slice. The times are simulated.
256 devices in a mesh: seq: 8 (over z), nbr: 32 (over y, x, core).
Axes of the slice: x: 4, y: 4, z: 8, core: 2. Of those that a mesh axis runs over, the one named last changes fastest.
Arguments:
- queries: bfloat16 [32768, 2048], P(('seq', 'nbr')), may hold values from -360 to 360
- d_context: bfloat16 [32768, 2048], P(('seq', 'nbr')), may hold values from -6 to 6
- database: bfloat16 [1024, 128, 1024], P(('seq', 'nbr')), may hold values from -6 to 6
- neighbour_source: int32 [512, 2], P(('seq', 'nbr')), may hold values from 0 to 7, all different within a row; in each aligned block of 2 rows (0 to 1, 2 to 3, ...) at most 2 rows name the same one
- neighbour_slot: int32 [512, 2], P(('seq', 'nbr')), may hold values from 0 to 3
- enc_gain: float32 [1024], replicated, may hold values from 0.1 to 1.9
- kv_weight: bfloat16 [1024, 4096], P('nbr'), may hold values from -0.1875 to 0.1875
Outputs:
- context: bfloat16 [32768, 2048], P(('seq', 'nbr'))
- d_queries: bfloat16 [32768, 2048], P(('seq', 'nbr'))
- d_kv_weight: float32 [1024, 4096], P('nbr')
- d_database: float32 [1024, 128, 1024], P(('seq', 'nbr'))
Inputs may be any that keep to these rules, and one draw needn't show every extreme that they name: `neighbour_source`: A span's 2 neighbours lie on different devices; among the neighbours of one device's spans at most 2 lie on any one device, and exactly 2 on one device in some or all devices.
All inputs are finite; a program needn't handle non-finite values.
Results may differ from a plain program's by a relative error of at most 0.024.
The roundings to bfloat16 on the way count: a program that leaves them out, or rounds other values in their place, can miss the bound.
Values may be sent and summed in bfloat16 or wider, within the bound.
No kernel may reach another device: no remote copies, remote signals or barrier semaphores. Data moves between devices by JAX's collectives and lax.ppermute only.
A program may use at most 128 MiB of HBM per device.

v0:
```python
import jax
import jax.numpy as jnp
from jax import lax
from jax.sharding import PartitionSpec as P

HEAD_DIM = 128
K_NBR = 2
EPSILON = 1e-06


def norm_rows(field_rows, enc_gain):
    mean_square = jnp.mean(field_rows * field_rows, axis=-1, keepdims=True)
    return field_rows * lax.rsqrt(mean_square + EPSILON) * enc_gain


def body(queries, d_context, database, neighbour_source, neighbour_slot, enc_gain, kv_weight):
    seq_count = lax.axis_size("seq")
    span_count = neighbour_source.shape[0]
    request_count = span_count * K_NBR
    capacity = max(2, 4 * span_count // seq_count)
    stored_rows = database.shape[0]
    row_length = database.shape[1]
    feature_width = database.shape[2]
    scale_factor = HEAD_DIM ** (-0.5)
    source_ids = neighbour_source.reshape(request_count)
    slot_ids = neighbour_slot.reshape(request_count)
    position = jnp.arange(request_count, dtype=jnp.int32)
    earlier_same = (source_ids[:, None] == source_ids[None, :]) & (
        position[None, :] < position[:, None]
    )
    bucket_ids = source_ids * capacity + jnp.sum(earlier_same, axis=1)
    bucket_count = seq_count * capacity
    bucket_match = bucket_ids[:, None] == jnp.arange(bucket_count, dtype=jnp.int32)[None, :]
    wanted_slots = jnp.sum(jnp.where(bucket_match, slot_ids[:, None] + 1, 0), axis=0) - 1
    wanted_slots = wanted_slots.reshape(seq_count, capacity)
    requested = lax.all_to_all(wanted_slots, "seq", split_axis=0, concat_axis=0, tiled=True)
    present = requested >= 0
    picked = database[jnp.clip(requested, 0, stored_rows - 1)]
    picked = jnp.where(present[:, :, None, None], picked, jnp.zeros_like(picked))
    arrived = lax.all_to_all(picked, "seq", split_axis=0, concat_axis=0, tiled=True)
    fetched = arrived.reshape(bucket_count, row_length, feature_width)[bucket_ids]
    fetched_wide = fetched.astype(jnp.float32)
    normed = norm_rows(fetched_wide, enc_gain).astype(jnp.bfloat16)
    flat_normed = normed.reshape(request_count * row_length, feature_width)
    weight_full = lax.all_gather(kv_weight, "nbr", axis=0, tiled=True)
    kv_width = weight_full.shape[1] // 2
    head_count = kv_width // HEAD_DIM
    projected = jnp.dot(flat_normed, weight_full, preferred_element_type=jnp.float32).astype(
        jnp.bfloat16
    )
    key_rows = projected[:, :kv_width].reshape(span_count, K_NBR * row_length, head_count, HEAD_DIM)
    value_rows = projected[:, kv_width:].reshape(
        span_count, K_NBR * row_length, head_count, HEAD_DIM
    )
    span_length = queries.shape[0] // span_count
    query_blocks = queries.reshape(span_count, span_length, head_count, HEAD_DIM)
    grad_blocks = d_context.reshape(span_count, span_length, head_count, HEAD_DIM)
    scores = (
        jnp.einsum("cqhd,ckhd->chqk", query_blocks, key_rows, preferred_element_type=jnp.float32)
        * scale_factor
    )
    highest = jnp.max(scores, axis=-1, keepdims=True)
    expanded = jnp.exp(scores - highest)
    probs = expanded / jnp.sum(expanded, axis=-1, keepdims=True)
    probs_half = probs.astype(jnp.bfloat16)
    context = jnp.einsum(
        "chqk,ckhd->cqhd", probs_half, value_rows, preferred_element_type=jnp.float32
    )
    context = context.astype(jnp.bfloat16).reshape(queries.shape)
    d_probs = jnp.einsum(
        "cqhd,ckhd->chqk", grad_blocks, value_rows, preferred_element_type=jnp.float32
    )
    delta = jnp.sum(probs * d_probs, axis=-1, keepdims=True)
    d_scores = (probs * (d_probs - delta) * scale_factor).astype(jnp.bfloat16)
    d_queries = jnp.einsum(
        "chqk,ckhd->cqhd", d_scores, key_rows, preferred_element_type=jnp.float32
    )
    d_queries = d_queries.astype(jnp.bfloat16).reshape(queries.shape)
    d_keys = jnp.einsum(
        "chqk,cqhd->ckhd", d_scores, query_blocks, preferred_element_type=jnp.float32
    ).astype(jnp.bfloat16)
    d_values = jnp.einsum(
        "chqk,cqhd->ckhd", probs_half, grad_blocks, preferred_element_type=jnp.float32
    ).astype(jnp.bfloat16)
    token_count = request_count * row_length
    d_projected = jnp.concatenate(
        [d_keys.reshape(token_count, kv_width), d_values.reshape(token_count, kv_width)], axis=1
    )
    wide_part = lax.psum_scatter(
        lax.dot_general(
            flat_normed, d_projected, (((0,), (0,)), ((), ())), preferred_element_type=jnp.float32
        ).astype(jnp.bfloat16),
        "nbr",
        scatter_dimension=0,
        tiled=True,
    ).astype(jnp.float32)
    d_kv_weight = lax.psum(wide_part, "seq")
    d_normed = lax.dot_general(
        d_projected, weight_full, (((1,), (1,)), ((), ())), preferred_element_type=jnp.float32
    )
    unused, pullback = jax.vjp(lambda field_rows: norm_rows(field_rows, enc_gain), fetched_wide)
    d_fetched = pullback(d_normed.reshape(request_count, row_length, feature_width))[0].astype(
        jnp.bfloat16
    )
    packed = (
        jnp.zeros((bucket_count, row_length, feature_width), jnp.bfloat16)
        .at[bucket_ids]
        .set(d_fetched)
    )
    packed = packed.reshape(seq_count, capacity, row_length, feature_width)
    grads_in, slots_in = (
        lax.all_to_all(packed, "seq", split_axis=0, concat_axis=0, tiled=True),
        lax.all_to_all(wanted_slots, "seq", split_axis=0, concat_axis=0, tiled=True),
    )
    slot_match = (
        jnp.arange(stored_rows, dtype=jnp.int32)[:, None] == slots_in.reshape(bucket_count)[None, :]
    )
    d_database = jnp.einsum(
        "sb,blw->slw",
        slot_match.astype(jnp.bfloat16),
        grads_in.reshape(bucket_count, row_length, feature_width),
        preferred_element_type=jnp.float32,
    )
    return (context, d_queries, d_kv_weight, d_database)


def solution(mesh):
    return jax.shard_map(
        body,
        mesh=mesh,
        in_specs=(
            P(("seq", "nbr"), None),
            P(("seq", "nbr"), None),
            P(("seq", "nbr"), None, None),
            P(("seq", "nbr"), None),
            P(("seq", "nbr"), None),
            P(),
            P("nbr", None),
        ),
        out_specs=(
            P(("seq", "nbr"), None),
            P(("seq", "nbr"), None),
            P("nbr", None),
            P(("seq", "nbr"), None, None),
        ),
        check_vma=False,
    )
```

profile of v0, /device:TPU:30, one launch (start us, length us, event | category | flops | bytes accessed | tf_op | source)
XLA Modules:
  0.0 381.9 jit_solution(1486818155061373319)
XLA Ops:
  7.2 0.7 all-gather.2.cloned.1.call-update
  7.9 0.8 reshape.172
  8.7 0.7 broadcast_add_fusion
  9.8 15.9 %all_to_all.17 = s32[8,1,2]{2,1,0:T(1,128)S(1)} all-to-all(s32[8,1,2]{2,1,0:T(1,128)S(1)} %bitcast.146), channel_id=1, replica_groups=mesh['seq'=8,'nbr'=32] {'seq'}, dimensions={0} | all-to-all | bytes 128 | tf_op jit(solution)/shard_map/all_to_all | solution.py:36
  26.1 2.8 gather_fusion
  28.9 4.5 %broadcast_select_fusion = bf16[8,2,128,1024]{3,2,1,0:T(8,128)(2,1)} fusion(bf16[8,2,128,1024]{3,2,1,0:T(8,128)(2,1)} %bitcast.130, pred[8,2]{1,0:T(8,128)(4,1)S(1)} %copy.84), kind=kLoop, calls=%fused_computation.7 | loop fusion | flops 2097152 | bytes 8388624 | tf_op jit(solution)/shard_map/jit(_where)/select_n | solution.py:39
  33.5 4.7 %all-to-all-start.1 = ((bf16[8,2,128,1024]{3,2,1,0:T(8,128)(2,1)}), bf16[8,2,128,1024]{3,2,1,0:T(8,128)(2,1)}, u32[]{:S(2)}, u32[]{:S(2)}) async-start(bf16[8,2,128,1024]{3,2,1,0:T(8,128)(2,1)} %broadcast_select_fusion), calls=%async_computation.1 | async-start | bytes 8388608 | tf_op jit(solution)/shard_map/all_to_all | solution.py:40
  38.3 0.9 copy.103
  39.2 0.9 copy.106
  40.1 93.1 %all-to-all-done.1 = bf16[8,2,128,1024]{3,2,1,0:T(8,128)(2,1)} async-done(((bf16[8,2,128,1024]{3,2,1,0:T(8,128)(2,1)}), bf16[8,2,128,1024]{3,2,1,0:T(8,128)(2,1)}, u32[]{:S(2)}, u32[]{:S(2)}) %all-to-all-start.1) | async-done | bytes 4194336 | tf_op jit(solution)/shard_map/all_to_all | solution.py:40
  133.2 2.8 gather_fusion.1
  136.0 0.3 fusion.8
  136.3 0.3 fusion.10
  136.6 8.9 %convolution_convert_fusion.1 = bf16[512,4096]{1,0:T(8,128)(2,1)S(1)} fusion(bf16[512,1024]{1,0:T(8,128)(2,1)S(1)} %fusion.10, bf16[1024,4096]{1,0:T(8,128)(2,1)} %all-gather.2.cloned.1.call-done), kind=kOutput, calls=%fused_computation.6 | convolution fusion | flops 4297064448 | bytes 13631488 | tf_op jit(solution)/shard_map/dot_general | solution.py:48
  145.6 0.6 slice_bitcast_fusion.1
  146.2 0.6 copy.102
  146.8 0.6 copy.104
  147.4 0.7 copy-done.3
  148.2 0.8 fusion.21
  149.1 1.9 fusion.65
  151.1 2.2 fusion.15
  153.3 8.0 %convert_bitcast_fusion = bf16[2,256,16,128]{3,1,2,0:T(8,128)(2,1)} fusion(bf16[2,64,16,128]{3,2,1,0:T(8,128)(2,1)} %bitcast.139, f32[2,16,64]{2,1,0:T(8,128)S(1)} %get-tuple-element.28, f32[2,16,256,64]{2,3,1,0:T(8,128)} %copy-done.2), kind=kOutput, calls=%fused_computation.31 | convolution fusion | flops 137890048 | bytes 4726784 | tf_op jit(solution)/shard_map/chqk,cqhd->ckhd/dot_general | solution.py:82
  161.3 17.1 %convert_bitcast_fusion.1 = bf16[2,256,16,128]{3,1,2,0:T(8,128)(2,1)} fusion(f32[2,16,256,64]{2,3,1,0:T(8,128)} %fusion.15, bf16[2,64,16,128]{3,2,1,0:T(8,128)(2,1)} %bitcast.137, f32[2,16,64,256]{3,2,1,0:T(8,128)} %get-tuple-element.29, f32[2,16,64]{2,1,0:T(8,128)S(1)} %get-tuple-element.28), kind=kOutput, calls=%fused_computation.32 | convolution fusion | flops 138938624 | bytes 6823936 | tf_op jit(solution)/shard_map/chqk,cqhd->ckhd/dot_general | solution.py:79
  178.3 3.1 copy.96
  181.4 1.4 copy.98
  182.8 0.5 bitcast_dynamic-update-slice_fusion.1
  183.3 0.5 bitcast_dynamic-update-slice_fusion
  183.9 1.9 copy-done.10
  185.8 6.9 %convolution_convert_fusion = bf16[1024,4096]{1,0:T(8,128)(2,1)} fusion(bf16[512,1024]{1,0:T(8,128)(2,1)S(1)} %copy-done.9, bf16[512,4096]{1,0:T(8,128)(2,1)S(1)} %bitcast_dynamic-update-slice_fusion), kind=kOutput, calls=%fused_computation.5 | convolution fusion | flops 4299161600 | bytes 13631488 | tf_op jit(solution)/shard_map/dot_general | solution.py:90
  192.7 8.4 %fusion.11 = (f32[512]{0:T(512)S(1)}, f32[512,1024]{1,0:T(8,128)S(1)}) fusion(bf16[4,128,1024]{2,1,0:T(8,128)(2,1)S(1)} %gather_fusion.1, f32[1024]{0:T(1024)S(1)} %copy-done.13, bf16[512,4096]{1,0:T(8,128)(2,1)} %copy-done.10, bf16[1024,4096]{1,0:T(8,128)(2,1)} %all-gather.2.cloned.1.call-done), kind=kOutput, calls=%fused_computation.30 | convolution fusion | flops 4297063936 | bytes 15734784 | tf_op jit(solution)/shard_map/dot_general | solution.py:98
  201.1 1.6 fusion.2
  202.7 2.5 broadcast_in_dim.30
  205.2 2.9 scatter_fusion
  208.1 8.7 %copy.99 = bf16[8,2,128,1024]{3,1,2,0:T(2,128)(2,1)} copy(bf16[8,2,128,1024]{3,2,1,0:T(8,128)(2,1)} %bitcast.129) | data formatting | bytes 8388608 | tf_op jit(solution)/shard_map/reshape | solution.py:110
  216.7 4.9 %all-to-all-start.2 = ((bf16[8,2,128,1024]{3,1,2,0:T(2,128)(2,1)}), bf16[8,2,128,1024]{3,1,2,0:T(2,128)(2,1)}, u32[]{:S(2)}, u32[]{:S(2)}) async-start(bf16[8,2,128,1024]{3,1,2,0:T(2,128)(2,1)} %copy.99), calls=%async_computation.3 | async-start | bytes 8388608 | tf_op jit(solution)/shard_map/all_to_all | solution.py:112
  221.6 0.5 broadcast.219
  222.1 0.7 reduce.4
  222.9 15.8 %fusion.32 = bf16[2,64,16,128]{3,1,2,0:T(8,128)(2,1)S(1)} fusion(bf16[2,256,16,128]{3,2,1,0:T(8,128)(2,1)} %bitcast.134, f32[2,16,256,64]{2,3,1,0:T(8,128)} %fusion.15, f32[2,16,64,256]{3,2,1,0:T(8,128)} %get-tuple-element.29, f32[2,16,64]{2,1,0:T(8,128)S(1)} %get-tuple-element.28), kind=kOutput, calls=%fused_computation.45 | convolution fusion | flops 138152192 | bytes 6823936 | tf_op jit(solution)/shard_map/chqk,ckhd->cqhd/dot_general | solution.py:75
  238.7 0.4 copy.94
  239.0 6.7 %fusion.29 = bf16[2,64,16,128]{3,1,2,0:T(8,128)(2,1)} fusion(bf16[2,256,16,128]{3,2,1,0:T(8,128)(2,1)S(1)} %bitcast.132, f32[2,16,64]{2,1,0:T(8,128)S(1)} %get-tuple-element.28, f32[2,16,256,64]{2,3,1,0:T(8,128)} %copy-done.2), kind=kOutput, calls=%fused_computation.44 | convolution fusion | flops 137103616 | bytes 4726784 | tf_op jit(solution)/shard_map/chqk,ckhd->cqhd/dot_general | solution.py:66
  245.7 1.4 copy.90
  247.1 1.2 copy_bitcast_fusion
  248.3 69.9 %all-to-all-done.2 = bf16[8,2,128,1024]{3,1,2,0:T(2,128)(2,1)} async-done(((bf16[8,2,128,1024]{3,1,2,0:T(2,128)(2,1)}), bf16[8,2,128,1024]{3,1,2,0:T(2,128)(2,1)}, u32[]{:S(2)}, u32[]{:S(2)}) %all-to-all-start.2) | async-done | bytes 4194336 | tf_op jit(solution)/shard_map/all_to_all | solution.py:112
  318.2 8.9 %copy.100 = bf16[8,2,128,1024]{3,1,0,2:T(2,128)(2,1)} copy(bf16[8,2,128,1024]{3,1,2,0:T(2,128)(2,1)} %all-to-all-done.2) | data formatting | bytes 8388608 | tf_op jit(solution)/shard_map/all_to_all | solution.py:112
  327.1 7.2 %reshape.184 = bf16[16,128,1024]{2,0,1:T(8,128)(2,1)} reshape(bf16[8,2,128,1024]{3,1,0,2:T(2,128)(2,1)} %copy.100) | data formatting | bytes 8388608 | tf_op jit(solution)/shard_map/reshape | solution.py:121
  334.3 3.0 fusion.46
  337.4 2.5 copy.101
  339.9 34.9 %all-reduce.1 = f32[32,4096]{1,0:T(8,128)} all-reduce(bf16[32,4096]{1,0:T(8,128)(2,1)} %reduce-scatter.2.cloned.1.call-done), channel_id=1, replica_groups=mesh['seq'=8,'nbr'=32] {'seq'}, use_global_device_ids=true, to_apply=%region_7.8 | all-reduce | flops 131072 | bytes 786432 | tf_op jit(solution)/shard_map/psum | solution.py:97
  (53 shorter events, 1.4 us)
Async XLA Ops:
  7.2 19.0 %copy-start = (bf16[4,128,1024]{2,1,0:T(8,128)(2,1)S(1)}, bf16[4,128,1024]{2,1,0:T(8,128)(2,1)}, u32[]{:S(2)}) copy-start(bf16[4,128,1024]{2,1,0:T(8,128)(2,1)} %param.9) | copy-start | bytes 3145732
  7.2 129.5 %all-gather.2.cloned.1.call-start = ((), (), s32[]{:S(2)}) async-start(), calls=%async_computation.4 | async-start | bytes 8650752 | tf_op jit(solution)/shard_map/all_gather | solution.py:45
  33.4 4.7 %copy-start.14 = (s32[2,2]{1,0:T(2,128)S(1)}, s32[2,2]{1,0:T(2,128)}, u32[]{:S(2)}) copy-start(s32[2,2]{1,0:T(2,128)} %param.10) | copy-start | bytes 52
  33.4 4.8 %copy-start.11 = (bf16[128,2048]{1,0:T(8,128)(2,1)S(1)}, bf16[128,2048]{1,0:T(8,128)(2,1)}, u32[]{:S(2)}) copy-start(bf16[128,2048]{1,0:T(8,128)(2,1)} %param.7) | copy-start | bytes 1572868
  33.5 5.8 %copy-start.12 = (bf16[128,2048]{1,0:T(8,128)(2,1)S(1)}, bf16[128,2048]{1,0:T(8,128)(2,1)}, u32[]{:S(2)}) copy-start(bf16[128,2048]{1,0:T(8,128)(2,1)} %param.8) | copy-start | bytes 1572868
  33.5 99.7 %all-to-all-start.1 = ((bf16[8,2,128,1024]{3,2,1,0:T(8,128)(2,1)}), bf16[8,2,128,1024]{3,2,1,0:T(8,128)(2,1)}, u32[]{:S(2)}, u32[]{:S(2)}) async-start(bf16[8,2,128,1024]{3,2,1,0:T(8,128)(2,1)} %broadcast_select_fusion), calls=%async_computation.1 | async-start | bytes 8388608 | tf_op jit(solution)/shard_map/all_to_all | solution.py:40
  38.1 301.7 %reduce-scatter.2.cloned.1.call-start = ((), (), s32[]{:S(2)}) async-start(), calls=%async_computation.5 | async-start | bytes 8650752 | tf_op jit(solution)/shard_map/reduce_scatter | solution.py:89
  39.2 97.1 %copy-start.13 = (f32[1024]{0:T(1024)S(1)}, f32[1024]{0:T(1024)}, u32[]{:S(2)}) copy-start(f32[1024]{0:T(1024)} %param.12) | copy-start | bytes 12292
  136.6 8.9 %copy-start.8 = (bf16[512,1024]{1,0:T(8,128)(2,1)}, bf16[512,1024]{1,0:T(8,128)(2,1)S(1)}, u32[]{:S(2)}) copy-start(bf16[512,1024]{1,0:T(8,128)(2,1)S(1)} %fusion.10) | copy-start | bytes 3145732
  146.8 1.3 copy-start.3
  146.8 1.4 copy-start.5
  149.1 2.0 copy-start.2
  149.1 2.0 copy-start.6
  178.3 3.1 copy-start.7
  183.3 2.5 copy-start.9
  183.8 1.9 copy-start.10
  202.7 2.5 copy-start.4
  216.7 101.5 %all-to-all-start.2 = ((bf16[8,2,128,1024]{3,1,2,0:T(2,128)(2,1)}), bf16[8,2,128,1024]{3,1,2,0:T(2,128)(2,1)}, u32[]{:S(2)}, u32[]{:S(2)}) async-start(bf16[8,2,128,1024]{3,1,2,0:T(2,128)(2,1)} %copy.99), calls=%async_computation.3 | async-start | bytes 8388608 | tf_op jit(solution)/shard_map/all_to_all | solution.py:112
  334.3 40.5 %copy-start.1 = (bf16[4,128,1024]{2,1,0:T(8,128)(2,1)S(1)}, bf16[4,128,1024]{2,1,0:T(8,128)(2,1)}, u32[]{:S(2)}) copy-start(bf16[4,128,1024]{2,1,0:T(8,128)(2,1)} %param.9) | copy-start | bytes 3145732
Sparse Core Ops, SparseCore 0:
  10.6 58.6 all-gather.1
  192.8 94.1 reduce-scatter.1
where the time goes:
time: 386 us; the launch traced here: 382 us
  waiting for transfers between devices  164 us (42%)
  matrix products  77.8 us (20%)
  local copies, waits for them, and re-layouts  55.1 us (14%)
  blocking collectives  50.9 us (13%)
  between operations  14.5 us (4%)
  other arithmetic  10.3 us (3%)
  starting transfers between devices  9.62 us (2%)
    all_to_all x1, waiting for transfers between devices, body(): lax.all_to_all(picked, 'seq', split_axis=0, concat_axis=0, tiled=True)  93.1 us
    all_to_all x1, waiting for transfers between devices, body(): lax.all_to_all(packed, 'seq', split_axis=0, concat_axis=0, tiled=True)  69.9 us
    psum x1, blocking collectives, body(): d_kv_weight = lax.psum(wide_part, 'seq')  34.9 us
    dot_general x1, matrix products, body(): jnp.einsum('chqk,cqhd->ckhd', d_scores, query_blocks, preferred_element_t...  17.1 us
    all_to_all x1, blocking collectives, body(): lax.all_to_all(wanted_slots, 'seq', split_axis=0, concat_axis=0, tiled=True)  15.9 us
    dot_general x1, matrix products, body(): jnp.einsum('chqk,ckhd->cqhd', d_scores, key_rows, preferred_element_type=...  15.8 us
    unnamed x37, local copies, waits for them, and re-layouts  9.54 us
    dot_general x1, matrix products, body(): jnp.dot(flat_normed, weight_full, preferred_element_type=jnp.float32)  8.9 us
  transfers between devices with their start and end apart: 4, of which 2 were waited for; matrix products, arithmetic and copies ran while one was open for 23% of the time, Pallas kernels for 0%

commit v1 on v0

--- a/solution.py
+++ b/solution.py
@@ -94,7 +94,7 @@
         scatter_dimension=0,
         tiled=True,
     ).astype(jnp.float32)
-    d_kv_weight = lax.psum(wide_part, "seq")
+    d_kv_weight = jnp.sum(lax.all_gather(wide_part, "seq"), axis=0)
     d_normed = lax.dot_general(
         d_projected, weight_full, (((1,), (1,)), ((), ())), preferred_element_type=jnp.float32
     )

time: 386 us -> 372 us (0.964)
  blocking collectives: 50.9 us -> 15.9 us
  waiting for transfers between devices: 164 us -> 178 us
  other arithmetic: 10.3 us -> 15.3 us
    all_to_all x1, waiting for transfers between devices: 69.9 us -> 2.54 us  [body(): lax.all_to_all(packed, 'seq', split_axis=0, concat_axis=0, tiled=True)]
    reduce_scatter x1, waiting for transfers between devices: 0.01 us -> 65.6 us  [body(): lax.psum_scatter(lax.dot_general(flat_normed, d_projected, (((0,), (0,)),...]
    psum x1 -> x0, blocking collectives: 34.9 us -> none  [body(): d_kv_weight = lax.psum(wide_part, 'seq')]
    all_gather x0 -> x1, waiting for transfers between devices: none -> 16.5 us  [body(): d_kv_weight = jnp.sum(lax.all_gather(wide_part, 'seq'), axis=0)]
  transfers between devices with their start and end apart: 4 -> 5, of which waited for: 2 -> 4; matrix products, arithmetic and copies ran while one was open for 23% -> 24% of each run, Pallas kernels for 0% -> 0%
where the time goes in v1:
time: 372 us; the launch traced here: 366 us
  waiting for transfers between devices  178 us (48%)
  matrix products  77.4 us (21%)
  local copies, waits for them, and re-layouts  55.3 us (15%)
  blocking collectives  15.9 us (4%)
  other arithmetic  15.3 us (4%)
  between operations  14.2 us (4%)
  starting transfers between devices  9.57 us (3%)
    all_to_all x1, waiting for transfers between devices, body(): lax.all_to_all(picked, 'seq', split_axis=0, concat_axis=0, tiled=True)  93.1 us
    reduce_scatter x1, waiting for transfers between devices, body(): lax.psum_scatter(lax.dot_general(flat_normed, d_projected, (((0,), (0,)),...  65.6 us
    dot_general x1, matrix products, body(): jnp.einsum('chqk,cqhd->ckhd', d_scores, query_blocks, preferred_element_t...  17.1 us
    all_gather x1, waiting for transfers between devices, body(): d_kv_weight = jnp.sum(lax.all_gather(wide_part, 'seq'), axis=0)  16.5 us
    all_to_all x1, blocking collectives, body(): lax.all_to_all(wanted_slots, 'seq', split_axis=0, concat_axis=0, tiled=True)  15.9 us
    dot_general x1, matrix products, body(): jnp.einsum('chqk,ckhd->cqhd', d_scores, key_rows, preferred_element_type=...  15.3 us
    unnamed x37, local copies, waits for them, and re-layouts  9.54 us
    all_to_all x1, local copies, waits for them, and re-layouts, body(): lax.all_to_all(packed, 'seq', split_axis=0, concat_axis=0, tiled=True)  8.89 us
  transfers between devices with their start and end apart: 5, of which 4 were waited for; matrix products, arithmetic and copies ran while one was open for 24% of the time, Pallas kernels for 0%

profile of v1, /device:TPU:30, one launch (start us, length us, event | category | flops | bytes accessed | tf_op | source)
XLA Modules:
  0.0 366.3 jit_solution(14150702188123711842)
XLA Ops:
  7.2 0.7 all-gather.4.cloned.1.call-update
  7.9 0.8 reshape.172
  8.7 0.7 broadcast_add_fusion
  9.8 15.9 %all_to_all.17 = s32[8,1,2]{2,1,0:T(1,128)S(1)} all-to-all(s32[8,1,2]{2,1,0:T(1,128)S(1)} %bitcast.148), channel_id=1, replica_groups=mesh['seq'=8,'nbr'=32] {'seq'}, dimensions={0} | all-to-all | bytes 128 | tf_op jit(solution)/shard_map/all_to_all | solution.py:36
  26.1 2.8 gather_fusion
  28.9 4.6 %broadcast_select_fusion = bf16[8,2,128,1024]{3,2,1,0:T(8,128)(2,1)} fusion(bf16[8,2,128,1024]{3,2,1,0:T(8,128)(2,1)} %bitcast.131, pred[8,2]{1,0:T(8,128)(4,1)S(1)} %copy.84), kind=kLoop, calls=%fused_computation.7 | loop fusion | flops 2097152 | bytes 8388624 | tf_op jit(solution)/shard_map/jit(_where)/select_n | solution.py:39
  33.5 4.7 %all-to-all-start.1 = ((bf16[8,2,128,1024]{3,2,1,0:T(8,128)(2,1)}), bf16[8,2,128,1024]{3,2,1,0:T(8,128)(2,1)}, u32[]{:S(2)}, u32[]{:S(2)}) async-start(bf16[8,2,128,1024]{3,2,1,0:T(8,128)(2,1)} %broadcast_select_fusion), calls=%async_computation.1 | async-start | bytes 8388608 | tf_op jit(solution)/shard_map/all_to_all | solution.py:40
  38.4 0.9 copy.103
  39.3 0.9 copy.106
  40.2 93.1 %all-to-all-done.1 = bf16[8,2,128,1024]{3,2,1,0:T(8,128)(2,1)} async-done(((bf16[8,2,128,1024]{3,2,1,0:T(8,128)(2,1)}), bf16[8,2,128,1024]{3,2,1,0:T(8,128)(2,1)}, u32[]{:S(2)}, u32[]{:S(2)}) %all-to-all-start.1) | async-done | bytes 4194336 | tf_op jit(solution)/shard_map/all_to_all | solution.py:40
  133.3 2.8 gather_fusion.1
  136.7 8.7 %convolution_convert_fusion.1 = bf16[512,4096]{1,0:T(8,128)(2,1)S(1)} fusion(bf16[512,1024]{1,0:T(8,128)(2,1)S(1)} %fusion.10, bf16[1024,4096]{1,0:T(8,128)(2,1)} %all-gather.4.cloned.1.call-done), kind=kOutput, calls=%fused_computation.6 | convolution fusion | flops 4297064448 | bytes 13631488 | tf_op jit(solution)/shard_map/dot_general | solution.py:48
  145.5 0.6 slice_bitcast_fusion.1
  146.0 0.6 copy.102
  146.7 0.6 copy.104
  147.3 0.7 copy-done.3
  148.1 0.8 fusion.21
  149.0 1.9 fusion.65
  151.0 2.2 fusion.15
  153.2 8.0 %convert_bitcast_fusion = bf16[2,256,16,128]{3,1,2,0:T(8,128)(2,1)} fusion(bf16[2,64,16,128]{3,2,1,0:T(8,128)(2,1)} %bitcast.141, f32[2,16,64]{2,1,0:T(8,128)S(1)} %get-tuple-element.28, f32[2,16,256,64]{2,3,1,0:T(8,128)} %copy-done.2), kind=kOutput, calls=%fused_computation.31 | convolution fusion | flops 137890048 | bytes 4726784 | tf_op jit(solution)/shard_map/chqk,cqhd->ckhd/dot_general | solution.py:82
  161.2 17.1 %convert_bitcast_fusion.1 = bf16[2,256,16,128]{3,1,2,0:T(8,128)(2,1)} fusion(f32[2,16,256,64]{2,3,1,0:T(8,128)} %fusion.15, bf16[2,64,16,128]{3,2,1,0:T(8,128)(2,1)} %bitcast.139, f32[2,16,64,256]{3,2,1,0:T(8,128)} %get-tuple-element.29, f32[2,16,64]{2,1,0:T(8,128)S(1)} %get-tuple-element.28), kind=kOutput, calls=%fused_computation.32 | convolution fusion | flops 138938624 | bytes 6823936 | tf_op jit(solution)/shard_map/chqk,cqhd->ckhd/dot_general | solution.py:79
  178.3 3.1 copy.96
  181.4 1.4 copy.98
  182.7 0.5 bitcast_dynamic-update-slice_fusion.1
  183.3 0.5 bitcast_dynamic-update-slice_fusion
  183.8 1.9 copy-done.10
  185.7 7.2 %convolution_convert_fusion = bf16[1024,4096]{1,0:T(8,128)(2,1)} fusion(bf16[512,1024]{1,0:T(8,128)(2,1)S(1)} %copy-done.9, bf16[512,4096]{1,0:T(8,128)(2,1)S(1)} %bitcast_dynamic-update-slice_fusion), kind=kOutput, calls=%fused_computation.5 | convolution fusion | flops 4299161600 | bytes 13631488 | tf_op jit(solution)/shard_map/dot_general | solution.py:90
  193.0 8.4 %fusion.11 = (f32[512]{0:T(512)S(1)}, f32[512,1024]{1,0:T(8,128)S(1)}) fusion(bf16[4,128,1024]{2,1,0:T(8,128)(2,1)S(1)} %gather_fusion.1, f32[1024]{0:T(1024)S(1)} %copy-done.13, bf16[512,4096]{1,0:T(8,128)(2,1)} %copy-done.10, bf16[1024,4096]{1,0:T(8,128)(2,1)} %all-gather.4.cloned.1.call-done), kind=kOutput, calls=%fused_computation.30 | convolution fusion | flops 4297063936 | bytes 15734784 | tf_op jit(solution)/shard_map/dot_general | solution.py:98
  201.4 1.5 fusion.2
  202.9 2.5 broadcast_in_dim.30
  205.3 2.9 scatter_fusion
  208.2 8.6 %copy.99 = bf16[8,2,128,1024]{3,1,2,0:T(2,128)(2,1)} copy(bf16[8,2,128,1024]{3,2,1,0:T(8,128)(2,1)} %bitcast.130) | data formatting | bytes 8388608 | tf_op jit(solution)/shard_map/reshape | solution.py:110
  216.8 4.6 %all-to-all-start.2 = ((bf16[8,2,128,1024]{3,1,2,0:T(2,128)(2,1)}), bf16[8,2,128,1024]{3,1,2,0:T(2,128)(2,1)}, u32[]{:S(2)}, u32[]{:S(2)}) async-start(bf16[8,2,128,1024]{3,1,2,0:T(2,128)(2,1)} %copy.99), calls=%async_computation.3 | async-start | bytes 8388608 | tf_op jit(solution)/shard_map/all_to_all | solution.py:112
  221.6 65.6 %reduce-scatter.2.cloned.1.call-done = bf16[32,4096]{1,0:T(8,128)(2,1)} async-done(((bf16[1024,4096]{1,0:T(8,128)(2,1)}), bf16[32,4096]{1,0:T(8,128)(2,1)}) %reduce-scatter.2.cloned.1.call-update) | async-done | bytes 262160 | tf_op jit(solution)/shard_map/reduce_scatter | solution.py:89
  287.3 1.8 all_gather.16
  289.1 0.5 broadcast.219
  289.6 0.7 reduce.4
  290.3 15.3 %fusion.32 = bf16[2,64,16,128]{3,1,2,0:T(8,128)(2,1)S(1)} fusion(bf16[2,256,16,128]{3,2,1,0:T(8,128)(2,1)} %bitcast.135, f32[2,16,256,64]{2,3,1,0:T(8,128)} %fusion.15, f32[2,16,64,256]{3,2,1,0:T(8,128)} %get-tuple-element.29, f32[2,16,64]{2,1,0:T(8,128)S(1)} %get-tuple-element.28), kind=kOutput, calls=%fused_computation.45 | convolution fusion | flops 138152192 | bytes 6823936 | tf_op jit(solution)/shard_map/chqk,ckhd->cqhd/dot_general | solution.py:75
  306.0 6.7 %fusion.29 = bf16[2,64,16,128]{3,1,2,0:T(8,128)(2,1)} fusion(bf16[2,256,16,128]{3,2,1,0:T(8,128)(2,1)S(1)} %bitcast.133, f32[2,16,64]{2,1,0:T(8,128)S(1)} %get-tuple-element.28, f32[2,16,256,64]{2,3,1,0:T(8,128)} %copy-done.2), kind=kOutput, calls=%fused_computation.44 | convolution fusion | flops 137103616 | bytes 4726784 | tf_op jit(solution)/shard_map/chqk,ckhd->cqhd/dot_general | solution.py:66
  312.6 1.4 copy.90
  314.0 1.2 copy_bitcast_fusion
  315.2 2.5 all-to-all-done.2
  317.8 8.9 %copy.100 = bf16[8,2,128,1024]{3,1,0,2:T(2,128)(2,1)} copy(bf16[8,2,128,1024]{3,1,2,0:T(2,128)(2,1)} %all-to-all-done.2) | data formatting | bytes 8388608 | tf_op jit(solution)/shard_map/all_to_all | solution.py:112
  326.7 7.5 %reshape.184 = bf16[16,128,1024]{2,0,1:T(8,128)(2,1)} reshape(bf16[8,2,128,1024]{3,1,0,2:T(2,128)(2,1)} %copy.100) | data formatting | bytes 8388608 | tf_op jit(solution)/shard_map/reshape | solution.py:121
  334.1 3.0 fusion.46
  337.1 2.5 copy.101
  339.6 16.5 %all-gather.6.cloned.1.call-done = f32[256,4096]{1,0:T(8,128)} async-done(((f32[32,4096]{1,0:T(8,128)}), f32[256,4096]{1,0:T(8,128)}) %all-gather.6.cloned.1.call-update) | async-done | bytes 4194320 | tf_op jit(solution)/shard_map/all_gather | solution.py:97
  356.2 3.3 reduce_sum.81
  (57 shorter events, 2.6 us)
Async XLA Ops:
  7.2 19.0 %copy-start = (bf16[4,128,1024]{2,1,0:T(8,128)(2,1)S(1)}, bf16[4,128,1024]{2,1,0:T(8,128)(2,1)}, u32[]{:S(2)}) copy-start(bf16[4,128,1024]{2,1,0:T(8,128)(2,1)} %param.9) | copy-start | bytes 3145732
  7.2 129.5 %all-gather.4.cloned.1.call-start = ((), (), s32[]{:S(2)}) async-start(), calls=%async_computation.4 | async-start | bytes 8650752 | tf_op jit(solution)/shard_map/all_gather | solution.py:45
  33.5 4.8 %copy-start.14 = (s32[2,2]{1,0:T(2,128)S(1)}, s32[2,2]{1,0:T(2,128)}, u32[]{:S(2)}) copy-start(s32[2,2]{1,0:T(2,128)} %param.10) | copy-start | bytes 52
  33.5 4.9 %copy-start.11 = (bf16[128,2048]{1,0:T(8,128)(2,1)S(1)}, bf16[128,2048]{1,0:T(8,128)(2,1)}, u32[]{:S(2)}) copy-start(bf16[128,2048]{1,0:T(8,128)(2,1)} %param.7) | copy-start | bytes 1572868
  33.5 5.8 %copy-start.12 = (bf16[128,2048]{1,0:T(8,128)(2,1)S(1)}, bf16[128,2048]{1,0:T(8,128)(2,1)}, u32[]{:S(2)}) copy-start(bf16[128,2048]{1,0:T(8,128)(2,1)} %param.8) | copy-start | bytes 1572868
  33.5 99.8 %all-to-all-start.1 = ((bf16[8,2,128,1024]{3,2,1,0:T(8,128)(2,1)}), bf16[8,2,128,1024]{3,2,1,0:T(8,128)(2,1)}, u32[]{:S(2)}, u32[]{:S(2)}) async-start(bf16[8,2,128,1024]{3,2,1,0:T(8,128)(2,1)} %broadcast_select_fusion), calls=%async_computation.1 | async-start | bytes 8388608 | tf_op jit(solution)/shard_map/all_to_all | solution.py:40
  38.2 249.0 %reduce-scatter.2.cloned.1.call-start = ((), (), s32[]{:S(2)}) async-start(), calls=%async_computation.5 | async-start | bytes 8650752 | tf_op jit(solution)/shard_map/reduce_scatter | solution.py:89
  39.3 97.1 %copy-start.13 = (f32[1024]{0:T(1024)S(1)}, f32[1024]{0:T(1024)}, u32[]{:S(2)}) copy-start(f32[1024]{0:T(1024)} %param.12) | copy-start | bytes 12292
  136.7 8.8 %copy-start.8 = (bf16[512,1024]{1,0:T(8,128)(2,1)}, bf16[512,1024]{1,0:T(8,128)(2,1)S(1)}, u32[]{:S(2)}) copy-start(bf16[512,1024]{1,0:T(8,128)(2,1)S(1)} %fusion.10) | copy-start | bytes 3145732
  146.7 1.3 copy-start.3
  146.7 1.4 copy-start.5
  149.0 2.0 copy-start.2
  149.0 2.0 copy-start.6
  178.3 3.1 copy-start.7
  183.3 2.5 copy-start.9
  183.8 1.9 copy-start.10
  202.9 2.5 copy-start.4
  216.8 100.9 %all-to-all-start.2 = ((bf16[8,2,128,1024]{3,1,2,0:T(2,128)(2,1)}), bf16[8,2,128,1024]{3,1,2,0:T(2,128)(2,1)}, u32[]{:S(2)}, u32[]{:S(2)}) async-start(bf16[8,2,128,1024]{3,1,2,0:T(2,128)(2,1)} %copy.99), calls=%async_computation.3 | async-start | bytes 8388608 | tf_op jit(solution)/shard_map/all_to_all | solution.py:112
  221.4 134.8 %all-gather.6.cloned.1.call-start = ((), (), s32[]{:S(2)}) async-start(), calls=%async_computation.6 | async-start | bytes 4718592 | tf_op jit(solution)/shard_map/all_gather | solution.py:97
  356.2 3.3 copy-start.1
Sparse Core Ops, SparseCore 0:
  10.6 58.6 all-gather.3
  193.1 94.1 reduce-scatter.1
  289.2 66.9 all-gather.5
